TPU v7x, 128 devices: a whole 4x4x4 slice. The times are simulated.
128 devices in a mesh: gx: 16 (over y, z_lo, core), gy: 8 (over x, z_hi).
Axes of the slice: x: 4, y: 4, z: 4 (z_hi: 2, z_lo: 2; z = z_hi * 2 + z_lo), core: 2. Of those that a mesh axis runs over, the one named last changes fastest.
Arguments:
- thermal_anomaly_grid: float32 [30, 256, 2048], P(None, 'gy', 'gx'), may hold values from -5 to 5
- relative_moisture: float32 [30, 256, 2048], P(None, 'gy', 'gx'), may hold values from 0.05 to 1
- overcast_share: float32 [30, 256, 2048], P(None, 'gy', 'gx'), may hold values from 0 to 1
- sun_angle_projection: float32 [256, 2048], P('gy', 'gx'), may hold values from 0.1 to 1
- daylight_mask: int32 [16, 256], P('gx', 'gy'), may hold values 0 or 1
- radiator_owner_position: int32 [16, 256, 1], P('gx', 'gy'), may hold values from 0 to 15; in each aligned block of 32 rows (0 to 31, 32 to 63, ..., all dimensions but the last counted through in order) at most 4 rows name the same one
- molecular_opacity_lookup: bfloat16 [30, 140, 128], replicated, may hold values from 0.019897461 to 1.5
- condensed_opacity_per_share: float32 [140], replicated, may hold values from 0.05 to 1
- planck_emission_factor: float32 [140], replicated, may hold values from 0.2 to 1
- insolation_quadrature_factor: float32 [140], replicated, may hold values from 0.2 to 2
Outputs:
- advanced_anomaly_grid: float32 [30, 256, 2048], P(None, 'gy', 'gx')
- humidity_next: float32 [30, 256, 2048], P(None, 'gy', 'gx')
- ground_irradiance_slots: float32 [8, 16, 16, 4, 128], P('gy', 'gx')
Inputs may be any that keep to these rules, and one draw needn't show every extreme that they name: `radiator_owner_position`: among the 32 blocks of one device, at most 4 name the same host, and some device's blocks name one host exactly 4 times.
All inputs are finite; a program needn't handle non-finite values. No bound on the sum of `daylight_mask` on one device may be relied on, other than what follows from the above.
Results may differ from a plain program's by a relative error of at most 0.0034.
Values may be sent and summed in bfloat16 or wider, within the bound.
A program may use at most 128 MiB of HBM per device.

v0:
```python
import jax
import jax.numpy as jnp
from jax import lax
from jax.sharding import PartitionSpec as P

NT = 16
NQ = 8
diffusion = 0.2
diffusivity = 1.66


def extended(block, sides, width):
    for axis, dim in sides:
        count = lax.axis_size(axis)
        forward = [(i, i + 1) for i in range(count - 1)]
        backward = [(target, source) for source, target in forward]
        low = lax.ppermute(
            lax.slice_in_dim(block, block.shape[dim] - width, None, axis=dim), axis, forward
        )
        high = lax.ppermute(lax.slice_in_dim(block, 0, width, axis=dim), axis, backward)
        block = jnp.concatenate([low, block, high], axis=dim)
    return block


def stencil(bordered_grid):
    centre = bordered_grid[:, :, 1:-1, 1:-1]
    beside_all = (
        bordered_grid[:, :, 2:, 1:-1]
        + bordered_grid[:, :, :-2, 1:-1]
        + bordered_grid[:, :, 1:-1, 2:]
        + bordered_grid[:, :, 1:-1, :-2]
    )
    return centre + diffusion * (beside_all - 4.0 * centre)


def optical_depth(layer, table_layer, condensed_opacity_per_share):
    air_temp, moisture, condensate = (layer[0], layer[1], layer[2])
    temp_nodes = jnp.arange(NT, dtype=jnp.float32)
    humid_nodes = jnp.arange(NQ, dtype=jnp.float32)
    temp_pos = jnp.clip((air_temp + 3.0) * ((NT - 1.0) / 6.0), 0.0, NT - 1.0)
    humid_pos = jnp.clip(moisture * (NQ - 1.0), 0.0, NQ - 1.0)
    temp_hat = jnp.maximum(0.0, 1.0 - jnp.abs(temp_pos[None, :] - temp_nodes[:, None]))
    humid_hat = jnp.maximum(0.0, 1.0 - jnp.abs(humid_pos[None, :] - humid_nodes[:, None]))
    weights = (
        (temp_hat[:, None, :] * humid_hat[None, :, :]).reshape(NT * NQ, -1).astype(jnp.bfloat16)
    )
    gas_depth = jnp.dot(table_layer, weights, preferred_element_type=jnp.float32)
    return gas_depth + condensed_opacity_per_share[:, None] * condensate[None, :]


def column_physics(
    prognostic_bundle,
    zenith,
    incident,
    molecular_opacity_lookup,
    condensed_opacity_per_share,
    planck_emission_factor,
    insolation_quadrature_factor,
):
    layers = jnp.transpose(prognostic_bundle, (1, 0, 2))
    gpoints = planck_emission_factor.shape[0]

    def downward(carry, inputs):
        long_down, short_down = carry
        layer, table_layer = inputs
        depth = optical_depth(layer, table_layer, condensed_opacity_per_share)
        through = jnp.exp(-diffusivity * depth)
        source = planck_emission_factor[:, None] * (1.0 + 0.25 * layer[0][None, :])
        long_next = long_down * through + (1.0 - through) * source
        short_next = short_down * jnp.exp(-depth / zenith[None, :])
        gained = jnp.sum(long_down - long_next + short_down - short_next, axis=0)
        return ((long_next, short_next), gained)

    def upward(long_up, inputs):
        layer, table_layer = inputs
        depth = optical_depth(layer, table_layer, condensed_opacity_per_share)
        through = jnp.exp(-diffusivity * depth)
        source = planck_emission_factor[:, None] * (1.0 + 0.25 * layer[0][None, :])
        long_next = long_up * through + (1.0 - through) * source
        return (long_next, jnp.sum(long_up - long_next, axis=0))

    start_long = jnp.zeros((gpoints, prognostic_bundle.shape[2]), jnp.float32)
    start_short = insolation_quadrature_factor[:, None] * incident[None, :]
    bottom, down_gain = lax.scan(
        downward, (start_long, start_short), (layers, molecular_opacity_lookup)
    )
    start_up = planck_emission_factor[:, None] * (1.0 + 0.25 * layers[-1, 0][None, :])
    top_up, up_gain = lax.scan(upward, start_up, (layers, molecular_opacity_lookup), reverse=True)
    heating = 2.0 / gpoints * (down_gain + up_gain)
    ground_irradiance_result = jnp.sum(bottom[0] + bottom[1], axis=0) / gpoints
    return (heating, ground_irradiance_result)


def block_rank(hosts):
    profile_groups = hosts.shape[-1]
    earlier = jnp.arange(profile_groups)[None, :] < jnp.arange(profile_groups)[:, None]
    same = hosts[..., :, None] == hosts[..., None, :]
    return jnp.sum(jnp.logical_and(same, earlier), axis=-1)


def slot_table(hosts, host_ids, capacity):
    rank = block_rank(hosts)
    slot_ids = jnp.arange(capacity, dtype=jnp.int32)[None, :, None]
    chosen = jnp.logical_and(
        hosts[..., None, None, :] == host_ids[:, None, None], rank[..., None, None, :] == slot_ids
    )
    return chosen.astype(jnp.float32)


def radiate(
    received_state,
    received_light,
    molecular_opacity_lookup,
    condensed_opacity_per_share,
    planck_emission_factor,
    insolation_quadrature_factor,
):
    sources, items = (received_state.shape[0], received_state.shape[1])
    level_count, width = (received_state.shape[3], received_state.shape[4])
    columns = sources * items * width
    prognostic_bundle = (
        jnp.transpose(received_state, (2, 3, 0, 1, 4))
        .reshape(3, level_count, columns)
        .astype(jnp.float32)
    )
    shine = jnp.transpose(received_light, (2, 0, 1, 3)).reshape(2, columns).astype(jnp.float32)
    occupied = shine[0] > 0.0
    zenith = jnp.where(occupied, shine[0], 1.0)
    heating, ground_irradiance_result = column_physics(
        prognostic_bundle,
        zenith,
        shine[1],
        molecular_opacity_lookup,
        condensed_opacity_per_share,
        planck_emission_factor,
        insolation_quadrature_factor,
    )
    ground_irradiance_result = jnp.where(occupied, ground_irradiance_result, 0.0)
    heating = jnp.transpose(heating.reshape(level_count, sources, items, width), (1, 2, 0, 3))
    return (heating, ground_irradiance_result.reshape(sources, items, width))


def on_device(
    thermal_anomaly_grid,
    relative_moisture,
    overcast_share,
    sun_angle_projection,
    daylight_mask,
    radiator_owner_position,
    molecular_opacity_lookup,
    condensed_opacity_per_share,
    planck_emission_factor,
    insolation_quadrature_factor,
):
    host_count = lax.axis_size("gx")
    profile_groups = thermal_anomaly_grid.shape[1]
    capacity = max(2, (2 * profile_groups + host_count - 1) // host_count)
    bordered_grid = extended(
        jnp.stack((thermal_anomaly_grid, relative_moisture)), (("gx", 3), ("gy", 2)), 1
    )
    laplacian_blurred_grid = stencil(bordered_grid)
    prognostic_bundle = jnp.stack((thermal_anomaly_grid, relative_moisture, overcast_share)).astype(
        jnp.bfloat16
    )
    lit_rows = daylight_mask[0].astype(jnp.float32)[:, None]
    light = jnp.stack((sun_angle_projection, sun_angle_projection * lit_rows)).astype(jnp.bfloat16)
    own_hosts = radiator_owner_position[0, :, 0]
    slot_position = own_hosts * capacity + block_rank(own_hosts)
    every_state, every_light, every_host = (
        lax.all_gather(prognostic_bundle[None], "gx", axis=0, tiled=True),
        lax.all_gather(light[None], "gx", axis=0, tiled=True),
        lax.all_gather(own_hosts[None], "gx", axis=0, tiled=True),
    )
    mine = jnp.reshape(lax.axis_index("gx"), (1,))
    chooser = slot_table(every_host, mine, capacity)[:, 0].astype(jnp.bfloat16)
    received_state = jnp.einsum(
        "skb,sclbx->skclx", chooser, every_state, preferred_element_type=jnp.float32
    ).astype(jnp.bfloat16)
    received_light = jnp.einsum(
        "skb,scbx->skcx", chooser, every_light, preferred_element_type=jnp.float32
    ).astype(jnp.bfloat16)
    heating, ground_irradiance_result = radiate(
        received_state,
        received_light,
        molecular_opacity_lookup,
        condensed_opacity_per_share,
        planck_emission_factor,
        insolation_quadrature_factor,
    )
    returned = lax.all_to_all(heating, "gx", split_axis=0, concat_axis=0, tiled=True)
    flat_returned = returned.reshape(
        returned.shape[0] * returned.shape[1], returned.shape[2], returned.shape[3]
    )
    own_warming_rates = jnp.transpose(flat_returned[slot_position], (1, 0, 2))
    advanced_anomaly_grid = laplacian_blurred_grid[0] + own_warming_rates
    return (advanced_anomaly_grid, laplacian_blurred_grid[1], ground_irradiance_result[None, None])


def solution(mesh):
    placed = (
        P(None, "gy", "gx"),
        P(None, "gy", "gx"),
        P(None, "gy", "gx"),
        P("gy", "gx"),
        P("gx", "gy"),
        P("gx", "gy", None),
        P(),
        P(),
        P(),
        P(),
    )
    return jax.shard_map(
        on_device,
        mesh=mesh,
        in_specs=placed,
        out_specs=(P(None, "gy", "gx"), P(None, "gy", "gx"), P("gy", "gx", None, None, None)),
        check_vma=False,
    )
```

profile of v0, /device:TPU:1, one launch (start us, length us, event | category | flops | bytes accessed | tf_op | source)
XLA Modules:
  0.0 643.7 jit_solution(1116959172714404542)
XLA Ops:
  19.9 20.2 %all-gather = s32[16,32,1]{1,2,0:T(1,128)S(1)} all-gather(s32[1,32,1]{1,2,0:T(1,128)S(1)} %copy-done.6), channel_id=2, replica_groups=mesh['gx'=16,'gy'=8] {'gx'}, dimensions={0}, use_global_device_ids=true | all-gather | bytes 2176 | tf_op jit(solution)/shard_map/all_gather | solution.py:172
  40.8 17.3 %all_gather.10 = bf16[16,2,32,128]{3,2,1,0:T(8,128)(2,1)S(1)} all-gather(bf16[1,2,32,128]{3,2,1,0:T(8,128)(2,1)S(1)} %pad_maximum_fusion.18), channel_id=1, replica_groups=mesh['gx'=16,'gy'=8] {'gx'}, dimensions={0}, use_global_device_ids=true | all-gather | bytes 278528 | tf_op jit(solution)/shard_map/all_gather | solution.py:171
  64.5 5.8 collective-permute-start.3
  76.5 11.5 %all-gather.3.cloned.1.call-done = bf16[16,3,30,32,128]{4,3,2,1,0:T(8,128)(2,1)} async-done(((bf16[1,3,30,32,128]{4,3,2,1,0:T(8,128)(2,1)}), bf16[16,3,30,32,128]{4,3,2,1,0:T(8,128)(2,1)}) %all-gather.3.cloned.1.call-update) | async-done | bytes 11796496 | tf_op jit(solution)/shard_map/all_gather | solution.py:170
  88.0 6.0 convert_bitcast_fusion
  106.1 214.3 %while.31 = (s32[]{:T(128)}, f32[140,8192]{1,0:T(8,128)}, f32[30,8192]{1,0:T(8,128)S(1)}, bf16[30,140,128]{2,1,0:T(8,128)(2,1)}, f32[30,3,8192]{2,1,0:T(4,128)},...) while((s32[]{:T(128)}, f32[140,8192]{1,0:T(8,128)}, ...), condition=%wide.region_6.7_spmd, body=%wide.region_4.6_spmd.sunk | while | flops 308002816 | bytes 11375885 | solution.py:88
  107.4 5.6 subtract_reduce_fusion.4
  114.6 5.6 subtract_reduce_fusion.4
  136.0 5.6 subtract_reduce_fusion.4
  143.2 5.6 subtract_reduce_fusion.4
  150.3 5.6 subtract_reduce_fusion.4
  157.4 5.6 subtract_reduce_fusion.4
  164.6 5.6 subtract_reduce_fusion.4
  171.7 5.6 subtract_reduce_fusion.4
  178.9 5.6 subtract_reduce_fusion.4
  186.0 5.6 subtract_reduce_fusion.4
  193.2 5.6 subtract_reduce_fusion.4
  200.3 5.6 subtract_reduce_fusion.4
  207.4 5.6 subtract_reduce_fusion.4
  214.6 5.6 subtract_reduce_fusion.4
  221.7 5.6 subtract_reduce_fusion.4
  236.0 5.6 subtract_reduce_fusion.4
  243.2 5.6 subtract_reduce_fusion.4
  250.3 5.6 subtract_reduce_fusion.4
  257.4 5.6 subtract_reduce_fusion.4
  264.6 5.6 subtract_reduce_fusion.4
  271.7 5.6 subtract_reduce_fusion.4
  278.9 5.6 subtract_reduce_fusion.4
  286.0 5.6 subtract_reduce_fusion.4
  293.1 5.6 subtract_reduce_fusion.4
  300.3 5.6 subtract_reduce_fusion.4
  314.6 5.6 subtract_reduce_fusion.4
  320.5 293.4 %while.32 = (s32[]{:T(128)}, f32[140,8192]{1,0:T(8,128)}, f32[140,8192]{1,0:T(8,128)}, f32[30,8192]{1,0:T(8,128)S(1)}, bf16[30,140,128]{2,1,0:T(8,128)(2,1)}, /*...) while((s32[]{:T(128)}, f32[140,8192]{1,0:T(8,128)}, ...), condition=%wide.region_3.4_spmd.clone, body=%wide.region_1.3_spmd.clone.sunk | while | flops 314884096 | bytes 20714776 | solution.py:84
  321.8 7.6 %subtract_reduce_fusion.5 = (f32[8192]{0:T(1024)S(1)}, f32[140,8192]{1,0:T(8,128)}, f32[140,8192]{1,0:T(8,128)}) fusion(f32[140,8192]{1,0:T(8,128)} %get-tuple-element.499, f32[140,8192]{1,0:T(8,128)} %get-tuple-element.498, pred[]{:T(512)S(6)} %compare.3, f32[8192]{0:T(1024)S(1)} %get-tuple-element.518, f32[8192]{0:T(1024)S(1)} %bitcast.125, ...), kind=kOutput, calls=%fused_computation.21.clone.1 | convolution fusion | flops 314040320 | bytes 19567716 | tf_op jit(solution)/shard_map/while/body/eval_jaxpr/dot_general | solution.py:47
  331.0 8.3 %subtract_reduce_fusion.5 = (f32[8192]{0:T(1024)S(1)}, f32[140,8192]{1,0:T(8,128)}, f32[140,8192]{1,0:T(8,128)}) fusion(f32[140,8192]{1,0:T(8,128)} %get-tuple-element.499, f32[140,8192]{1,0:T(8,128)} %get-tuple-element.498, pred[]{:T(512)S(6)} %compare.3, f32[8192]{0:T(1024)S(1)} %get-tuple-element.518, f32[8192]{0:T(1024)S(1)} %bitcast.125, ...), kind=kOutput, calls=%fused_computation.21.clone.1 | convolution fusion | flops 314040320 | bytes 19567716 | tf_op jit(solution)/shard_map/while/body/eval_jaxpr/dot_general | solution.py:47
  340.8 8.3 %subtract_reduce_fusion.5 = (f32[8192]{0:T(1024)S(1)}, f32[140,8192]{1,0:T(8,128)}, f32[140,8192]{1,0:T(8,128)}) fusion(f32[140,8192]{1,0:T(8,128)} %get-tuple-element.499, f32[140,8192]{1,0:T(8,128)} %get-tuple-element.498, pred[]{:T(512)S(6)} %compare.3, f32[8192]{0:T(1024)S(1)} %get-tuple-element.518, f32[8192]{0:T(1024)S(1)} %bitcast.125, ...), kind=kOutput, calls=%fused_computation.21.clone.1 | convolution fusion | flops 314040320 | bytes 19567716 | tf_op jit(solution)/shard_map/while/body/eval_jaxpr/dot_general | solution.py:47
  350.6 8.3 %subtract_reduce_fusion.5 = (f32[8192]{0:T(1024)S(1)}, f32[140,8192]{1,0:T(8,128)}, f32[140,8192]{1,0:T(8,128)}) fusion(f32[140,8192]{1,0:T(8,128)} %get-tuple-element.499, f32[140,8192]{1,0:T(8,128)} %get-tuple-element.498, pred[]{:T(512)S(6)} %compare.3, f32[8192]{0:T(1024)S(1)} %get-tuple-element.518, f32[8192]{0:T(1024)S(1)} %bitcast.125, ...), kind=kOutput, calls=%fused_computation.21.clone.1 | convolution fusion | flops 314040320 | bytes 19567716 | tf_op jit(solution)/shard_map/while/body/eval_jaxpr/dot_general | solution.py:47
  360.4 8.3 %subtract_reduce_fusion.5 = (f32[8192]{0:T(1024)S(1)}, f32[140,8192]{1,0:T(8,128)}, f32[140,8192]{1,0:T(8,128)}) fusion(f32[140,8192]{1,0:T(8,128)} %get-tuple-element.499, f32[140,8192]{1,0:T(8,128)} %get-tuple-element.498, pred[]{:T(512)S(6)} %compare.3, f32[8192]{0:T(1024)S(1)} %get-tuple-element.518, f32[8192]{0:T(1024)S(1)} %bitcast.125, ...), kind=kOutput, calls=%fused_computation.21.clone.1 | convolution fusion | flops 314040320 | bytes 19567716 | tf_op jit(solution)/shard_map/while/body/eval_jaxpr/dot_general | solution.py:47
  370.2 8.3 %subtract_reduce_fusion.5 = (f32[8192]{0:T(1024)S(1)}, f32[140,8192]{1,0:T(8,128)}, f32[140,8192]{1,0:T(8,128)}) fusion(f32[140,8192]{1,0:T(8,128)} %get-tuple-element.499, f32[140,8192]{1,0:T(8,128)} %get-tuple-element.498, pred[]{:T(512)S(6)} %compare.3, f32[8192]{0:T(1024)S(1)} %get-tuple-element.518, f32[8192]{0:T(1024)S(1)} %bitcast.125, ...), kind=kOutput, calls=%fused_computation.21.clone.1 | convolution fusion | flops 314040320 | bytes 19567716 | tf_op jit(solution)/shard_map/while/body/eval_jaxpr/dot_general | solution.py:47
  380.0 8.3 %subtract_reduce_fusion.5 = (f32[8192]{0:T(1024)S(1)}, f32[140,8192]{1,0:T(8,128)}, f32[140,8192]{1,0:T(8,128)}) fusion(f32[140,8192]{1,0:T(8,128)} %get-tuple-element.499, f32[140,8192]{1,0:T(8,128)} %get-tuple-element.498, pred[]{:T(512)S(6)} %compare.3, f32[8192]{0:T(1024)S(1)} %get-tuple-element.518, f32[8192]{0:T(1024)S(1)} %bitcast.125, ...), kind=kOutput, calls=%fused_computation.21.clone.1 | convolution fusion | flops 314040320 | bytes 19567716 | tf_op jit(solution)/shard_map/while/body/eval_jaxpr/dot_general | solution.py:47
  389.8 8.3 %subtract_reduce_fusion.5 = (f32[8192]{0:T(1024)S(1)}, f32[140,8192]{1,0:T(8,128)}, f32[140,8192]{1,0:T(8,128)}) fusion(f32[140,8192]{1,0:T(8,128)} %get-tuple-element.499, f32[140,8192]{1,0:T(8,128)} %get-tuple-element.498, pred[]{:T(512)S(6)} %compare.3, f32[8192]{0:T(1024)S(1)} %get-tuple-element.518, f32[8192]{0:T(1024)S(1)} %bitcast.125, ...), kind=kOutput, calls=%fused_computation.21.clone.1 | convolution fusion | flops 314040320 | bytes 19567716 | tf_op jit(solution)/shard_map/while/body/eval_jaxpr/dot_general | solution.py:47
  399.6 8.3 %subtract_reduce_fusion.5 = (f32[8192]{0:T(1024)S(1)}, f32[140,8192]{1,0:T(8,128)}, f32[140,8192]{1,0:T(8,128)}) fusion(f32[140,8192]{1,0:T(8,128)} %get-tuple-element.499, f32[140,8192]{1,0:T(8,128)} %get-tuple-element.498, pred[]{:T(512)S(6)} %compare.3, f32[8192]{0:T(1024)S(1)} %get-tuple-element.518, f32[8192]{0:T(1024)S(1)} %bitcast.125, ...), kind=kOutput, calls=%fused_computation.21.clone.1 | convolution fusion | flops 314040320 | bytes 19567716 | tf_op jit(solution)/shard_map/while/body/eval_jaxpr/dot_general | solution.py:47
  409.4 8.3 %subtract_reduce_fusion.5 = (f32[8192]{0:T(1024)S(1)}, f32[140,8192]{1,0:T(8,128)}, f32[140,8192]{1,0:T(8,128)}) fusion(f32[140,8192]{1,0:T(8,128)} %get-tuple-element.499, f32[140,8192]{1,0:T(8,128)} %get-tuple-element.498, pred[]{:T(512)S(6)} %compare.3, f32[8192]{0:T(1024)S(1)} %get-tuple-element.518, f32[8192]{0:T(1024)S(1)} %bitcast.125, ...), kind=kOutput, calls=%fused_computation.21.clone.1 | convolution fusion | flops 314040320 | bytes 19567716 | tf_op jit(solution)/shard_map/while/body/eval_jaxpr/dot_general | solution.py:47
  419.2 8.3 %subtract_reduce_fusion.5 = (f32[8192]{0:T(1024)S(1)}, f32[140,8192]{1,0:T(8,128)}, f32[140,8192]{1,0:T(8,128)}) fusion(f32[140,8192]{1,0:T(8,128)} %get-tuple-element.499, f32[140,8192]{1,0:T(8,128)} %get-tuple-element.498, pred[]{:T(512)S(6)} %compare.3, f32[8192]{0:T(1024)S(1)} %get-tuple-element.518, f32[8192]{0:T(1024)S(1)} %bitcast.125, ...), kind=kOutput, calls=%fused_computation.21.clone.1 | convolution fusion | flops 314040320 | bytes 19567716 | tf_op jit(solution)/shard_map/while/body/eval_jaxpr/dot_general | solution.py:47
  429.0 8.3 %subtract_reduce_fusion.5 = (f32[8192]{0:T(1024)S(1)}, f32[140,8192]{1,0:T(8,128)}, f32[140,8192]{1,0:T(8,128)}) fusion(f32[140,8192]{1,0:T(8,128)} %get-tuple-element.499, f32[140,8192]{1,0:T(8,128)} %get-tuple-element.498, pred[]{:T(512)S(6)} %compare.3, f32[8192]{0:T(1024)S(1)} %get-tuple-element.518, f32[8192]{0:T(1024)S(1)} %bitcast.125, ...), kind=kOutput, calls=%fused_computation.21.clone.1 | convolution fusion | flops 314040320 | bytes 19567716 | tf_op jit(solution)/shard_map/while/body/eval_jaxpr/dot_general | solution.py:47
  438.8 8.3 %subtract_reduce_fusion.5 = (f32[8192]{0:T(1024)S(1)}, f32[140,8192]{1,0:T(8,128)}, f32[140,8192]{1,0:T(8,128)}) fusion(f32[140,8192]{1,0:T(8,128)} %get-tuple-element.499, f32[140,8192]{1,0:T(8,128)} %get-tuple-element.498, pred[]{:T(512)S(6)} %compare.3, f32[8192]{0:T(1024)S(1)} %get-tuple-element.518, f32[8192]{0:T(1024)S(1)} %bitcast.125, ...), kind=kOutput, calls=%fused_computation.21.clone.1 | convolution fusion | flops 314040320 | bytes 19567716 | tf_op jit(solution)/shard_map/while/body/eval_jaxpr/dot_general | solution.py:47
  448.6 8.3 %subtract_reduce_fusion.5 = (f32[8192]{0:T(1024)S(1)}, f32[140,8192]{1,0:T(8,128)}, f32[140,8192]{1,0:T(8,128)}) fusion(f32[140,8192]{1,0:T(8,128)} %get-tuple-element.499, f32[140,8192]{1,0:T(8,128)} %get-tuple-element.498, pred[]{:T(512)S(6)} %compare.3, f32[8192]{0:T(1024)S(1)} %get-tuple-element.518, f32[8192]{0:T(1024)S(1)} %bitcast.125, ...), kind=kOutput, calls=%fused_computation.21.clone.1 | convolution fusion | flops 314040320 | bytes 19567716 | tf_op jit(solution)/shard_map/while/body/eval_jaxpr/dot_general | solution.py:47
  458.4 8.3 %subtract_reduce_fusion.5 = (f32[8192]{0:T(1024)S(1)}, f32[140,8192]{1,0:T(8,128)}, f32[140,8192]{1,0:T(8,128)}) fusion(f32[140,8192]{1,0:T(8,128)} %get-tuple-element.499, f32[140,8192]{1,0:T(8,128)} %get-tuple-element.498, pred[]{:T(512)S(6)} %compare.3, f32[8192]{0:T(1024)S(1)} %get-tuple-element.518, f32[8192]{0:T(1024)S(1)} %bitcast.125, ...), kind=kOutput, calls=%fused_computation.21.clone.1 | convolution fusion | flops 314040320 | bytes 19567716 | tf_op jit(solution)/shard_map/while/body/eval_jaxpr/dot_general | solution.py:47
  468.2 8.3 %subtract_reduce_fusion.5 = (f32[8192]{0:T(1024)S(1)}, f32[140,8192]{1,0:T(8,128)}, f32[140,8192]{1,0:T(8,128)}) fusion(f32[140,8192]{1,0:T(8,128)} %get-tuple-element.499, f32[140,8192]{1,0:T(8,128)} %get-tuple-element.498, pred[]{:T(512)S(6)} %compare.3, f32[8192]{0:T(1024)S(1)} %get-tuple-element.518, f32[8192]{0:T(1024)S(1)} %bitcast.125, ...), kind=kOutput, calls=%fused_computation.21.clone.1 | convolution fusion | flops 314040320 | bytes 19567716 | tf_op jit(solution)/shard_map/while/body/eval_jaxpr/dot_general | solution.py:47
  478.0 8.3 %subtract_reduce_fusion.5 = (f32[8192]{0:T(1024)S(1)}, f32[140,8192]{1,0:T(8,128)}, f32[140,8192]{1,0:T(8,128)}) fusion(f32[140,8192]{1,0:T(8,128)} %get-tuple-element.499, f32[140,8192]{1,0:T(8,128)} %get-tuple-element.498, pred[]{:T(512)S(6)} %compare.3, f32[8192]{0:T(1024)S(1)} %get-tuple-element.518, f32[8192]{0:T(1024)S(1)} %bitcast.125, ...), kind=kOutput, calls=%fused_computation.21.clone.1 | convolution fusion | flops 314040320 | bytes 19567716 | tf_op jit(solution)/shard_map/while/body/eval_jaxpr/dot_general | solution.py:47
  487.8 8.3 %subtract_reduce_fusion.5 = (f32[8192]{0:T(1024)S(1)}, f32[140,8192]{1,0:T(8,128)}, f32[140,8192]{1,0:T(8,128)}) fusion(f32[140,8192]{1,0:T(8,128)} %get-tuple-element.499, f32[140,8192]{1,0:T(8,128)} %get-tuple-element.498, pred[]{:T(512)S(6)} %compare.3, f32[8192]{0:T(1024)S(1)} %get-tuple-element.518, f32[8192]{0:T(1024)S(1)} %bitcast.125, ...), kind=kOutput, calls=%fused_computation.21.clone.1 | convolution fusion | flops 314040320 | bytes 19567716 | tf_op jit(solution)/shard_map/while/body/eval_jaxpr/dot_general | solution.py:47
  497.6 8.3 %subtract_reduce_fusion.5 = (f32[8192]{0:T(1024)S(1)}, f32[140,8192]{1,0:T(8,128)}, f32[140,8192]{1,0:T(8,128)}) fusion(f32[140,8192]{1,0:T(8,128)} %get-tuple-element.499, f32[140,8192]{1,0:T(8,128)} %get-tuple-element.498, pred[]{:T(512)S(6)} %compare.3, f32[8192]{0:T(1024)S(1)} %get-tuple-element.518, f32[8192]{0:T(1024)S(1)} %bitcast.125, ...), kind=kOutput, calls=%fused_computation.21.clone.1 | convolution fusion | flops 314040320 | bytes 19567716 | tf_op jit(solution)/shard_map/while/body/eval_jaxpr/dot_general | solution.py:47
  507.4 8.3 %subtract_reduce_fusion.5 = (f32[8192]{0:T(1024)S(1)}, f32[140,8192]{1,0:T(8,128)}, f32[140,8192]{1,0:T(8,128)}) fusion(f32[140,8192]{1,0:T(8,128)} %get-tuple-element.499, f32[140,8192]{1,0:T(8,128)} %get-tuple-element.498, pred[]{:T(512)S(6)} %compare.3, f32[8192]{0:T(1024)S(1)} %get-tuple-element.518, f32[8192]{0:T(1024)S(1)} %bitcast.125, ...), kind=kOutput, calls=%fused_computation.21.clone.1 | convolution fusion | flops 314040320 | bytes 19567716 | tf_op jit(solution)/shard_map/while/body/eval_jaxpr/dot_general | solution.py:47
  517.2 8.3 %subtract_reduce_fusion.5 = (f32[8192]{0:T(1024)S(1)}, f32[140,8192]{1,0:T(8,128)}, f32[140,8192]{1,0:T(8,128)}) fusion(f32[140,8192]{1,0:T(8,128)} %get-tuple-element.499, f32[140,8192]{1,0:T(8,128)} %get-tuple-element.498, pred[]{:T(512)S(6)} %compare.3, f32[8192]{0:T(1024)S(1)} %get-tuple-element.518, f32[8192]{0:T(1024)S(1)} %bitcast.125, ...), kind=kOutput, calls=%fused_computation.21.clone.1 | convolution fusion | flops 314040320 | bytes 19567716 | tf_op jit(solution)/shard_map/while/body/eval_jaxpr/dot_general | solution.py:47
  527.0 8.3 %subtract_reduce_fusion.5 = (f32[8192]{0:T(1024)S(1)}, f32[140,8192]{1,0:T(8,128)}, f32[140,8192]{1,0:T(8,128)}) fusion(f32[140,8192]{1,0:T(8,128)} %get-tuple-element.499, f32[140,8192]{1,0:T(8,128)} %get-tuple-element.498, pred[]{:T(512)S(6)} %compare.3, f32[8192]{0:T(1024)S(1)} %get-tuple-element.518, f32[8192]{0:T(1024)S(1)} %bitcast.125, ...), kind=kOutput, calls=%fused_computation.21.clone.1 | convolution fusion | flops 314040320 | bytes 19567716 | tf_op jit(solution)/shard_map/while/body/eval_jaxpr/dot_general | solution.py:47
  536.8 8.3 %subtract_reduce_fusion.5 = (f32[8192]{0:T(1024)S(1)}, f32[140,8192]{1,0:T(8,128)}, f32[140,8192]{1,0:T(8,128)}) fusion(f32[140,8192]{1,0:T(8,128)} %get-tuple-element.499, f32[140,8192]{1,0:T(8,128)} %get-tuple-element.498, pred[]{:T(512)S(6)} %compare.3, f32[8192]{0:T(1024)S(1)} %get-tuple-element.518, f32[8192]{0:T(1024)S(1)} %bitcast.125, ...), kind=kOutput, calls=%fused_computation.21.clone.1 | convolution fusion | flops 314040320 | bytes 19567716 | tf_op jit(solution)/shard_map/while/body/eval_jaxpr/dot_general | solution.py:47
  546.6 8.3 %subtract_reduce_fusion.5 = (f32[8192]{0:T(1024)S(1)}, f32[140,8192]{1,0:T(8,128)}, f32[140,8192]{1,0:T(8,128)}) fusion(f32[140,8192]{1,0:T(8,128)} %get-tuple-element.499, f32[140,8192]{1,0:T(8,128)} %get-tuple-element.498, pred[]{:T(512)S(6)} %compare.3, f32[8192]{0:T(1024)S(1)} %get-tuple-element.518, f32[8192]{0:T(1024)S(1)} %bitcast.125, ...), kind=kOutput, calls=%fused_computation.21.clone.1 | convolution fusion | flops 314040320 | bytes 19567716 | tf_op jit(solution)/shard_map/while/body/eval_jaxpr/dot_general | solution.py:47
  556.4 8.3 %subtract_reduce_fusion.5 = (f32[8192]{0:T(1024)S(1)}, f32[140,8192]{1,0:T(8,128)}, f32[140,8192]{1,0:T(8,128)}) fusion(f32[140,8192]{1,0:T(8,128)} %get-tuple-element.499, f32[140,8192]{1,0:T(8,128)} %get-tuple-element.498, pred[]{:T(512)S(6)} %compare.3, f32[8192]{0:T(1024)S(1)} %get-tuple-element.518, f32[8192]{0:T(1024)S(1)} %bitcast.125, ...), kind=kOutput, calls=%fused_computation.21.clone.1 | convolution fusion | flops 314040320 | bytes 19567716 | tf_op jit(solution)/shard_map/while/body/eval_jaxpr/dot_general | solution.py:47
  566.2 8.3 %subtract_reduce_fusion.5 = (f32[8192]{0:T(1024)S(1)}, f32[140,8192]{1,0:T(8,128)}, f32[140,8192]{1,0:T(8,128)}) fusion(f32[140,8192]{1,0:T(8,128)} %get-tuple-element.499, f32[140,8192]{1,0:T(8,128)} %get-tuple-element.498, pred[]{:T(512)S(6)} %compare.3, f32[8192]{0:T(1024)S(1)} %get-tuple-element.518, f32[8192]{0:T(1024)S(1)} %bitcast.125, ...), kind=kOutput, calls=%fused_computation.21.clone.1 | convolution fusion | flops 314040320 | bytes 19567716 | tf_op jit(solution)/shard_map/while/body/eval_jaxpr/dot_general | solution.py:47
  576.0 8.3 %subtract_reduce_fusion.5 = (f32[8192]{0:T(1024)S(1)}, f32[140,8192]{1,0:T(8,128)}, f32[140,8192]{1,0:T(8,128)}) fusion(f32[140,8192]{1,0:T(8,128)} %get-tuple-element.499, f32[140,8192]{1,0:T(8,128)} %get-tuple-element.498, pred[]{:T(512)S(6)} %compare.3, f32[8192]{0:T(1024)S(1)} %get-tuple-element.518, f32[8192]{0:T(1024)S(1)} %bitcast.125, ...), kind=kOutput, calls=%fused_computation.21.clone.1 | convolution fusion | flops 314040320 | bytes 19567716 | tf_op jit(solution)/shard_map/while/body/eval_jaxpr/dot_general | solution.py:47
  585.8 8.3 %subtract_reduce_fusion.5 = (f32[8192]{0:T(1024)S(1)}, f32[140,8192]{1,0:T(8,128)}, f32[140,8192]{1,0:T(8,128)}) fusion(f32[140,8192]{1,0:T(8,128)} %get-tuple-element.499, f32[140,8192]{1,0:T(8,128)} %get-tuple-element.498, pred[]{:T(512)S(6)} %compare.3, f32[8192]{0:T(1024)S(1)} %get-tuple-element.518, f32[8192]{0:T(1024)S(1)} %bitcast.125, ...), kind=kOutput, calls=%fused_computation.21.clone.1 | convolution fusion | flops 314040320 | bytes 19567716 | tf_op jit(solution)/shard_map/while/body/eval_jaxpr/dot_general | solution.py:47
  595.6 8.3 %subtract_reduce_fusion.5 = (f32[8192]{0:T(1024)S(1)}, f32[140,8192]{1,0:T(8,128)}, f32[140,8192]{1,0:T(8,128)}) fusion(f32[140,8192]{1,0:T(8,128)} %get-tuple-element.499, f32[140,8192]{1,0:T(8,128)} %get-tuple-element.498, pred[]{:T(512)S(6)} %compare.3, f32[8192]{0:T(1024)S(1)} %get-tuple-element.518, f32[8192]{0:T(1024)S(1)} %bitcast.125, ...), kind=kOutput, calls=%fused_computation.21.clone.1 | convolution fusion | flops 314040320 | bytes 19567716 | tf_op jit(solution)/shard_map/while/body/eval_jaxpr/dot_general | solution.py:47
  605.4 8.3 %subtract_reduce_fusion.5 = (f32[8192]{0:T(1024)S(1)}, f32[140,8192]{1,0:T(8,128)}, f32[140,8192]{1,0:T(8,128)}) fusion(f32[140,8192]{1,0:T(8,128)} %get-tuple-element.499, f32[140,8192]{1,0:T(8,128)} %get-tuple-element.498, pred[]{:T(512)S(6)} %compare.3, f32[8192]{0:T(1024)S(1)} %get-tuple-element.518, f32[8192]{0:T(1024)S(1)} %bitcast.125, ...), kind=kOutput, calls=%fused_computation.21.clone.1 | convolution fusion | flops 314040320 | bytes 19567716 | tf_op jit(solution)/shard_map/while/body/eval_jaxpr/dot_general | solution.py:47
  627.1 7.8 %all-to-all-done = f32[16,4,30,128]{3,1,2,0:T(4,128)S(1)} async-done(((f32[16,4,30,128]{3,1,2,0:T(4,128)}), f32[16,4,30,128]{3,1,2,0:T(4,128)S(1)}, u32[]{:S(2)}, u32[]{:S(2)}) %all-to-all-start) | async-done | bytes 983072 | tf_op jit(solution)/shard_map/all_to_all | solution.py:190
  (316 shorter events, 164.0 us)
Async XLA Ops:
  7.2 3.5 copy-start.1
  7.2 3.5 copy-start.2
  7.2 80.8 %all-gather.3.cloned.1.call-start = ((), (), s32[]{:S(2)}) async-start(), calls=%async_computation.1 | async-start | bytes 12533760 | tf_op jit(solution)/shard_map/all_gather | solution.py:170
  9.6 10.2 %copy-start.6 = (s32[1,32,1]{1,2,0:T(1,128)S(1)}, s32[1,32,1]{1,2,0:T(1,128)}, u32[]{:S(2)}) copy-start(s32[1,32,1]{1,2,0:T(1,128)} %param.19) | copy-start | bytes 388
  9.7 30.4 %copy-start.8 = (s32[1,32]{1,0:T(1,128)S(1)}, s32[1,32]{1,0:T(1,128)}, u32[]{:S(2)}) copy-start(s32[1,32]{1,0:T(1,128)} %param.18) | copy-start | bytes 388
  9.7 30.4 %copy-start.3 = (f32[32,128]{1,0:T(8,128)S(1)}, f32[32,128]{1,0:T(8,128)}, u32[]{:S(2)}) copy-start(f32[32,128]{1,0:T(8,128)} %param.17) | copy-start | bytes 49156
  10.6 47.7 %copy-start.4 = (f32[140]{0:T(256)S(1)}, f32[140]{0:T(256)}, u32[]{:S(2)}) copy-start(f32[140]{0:T(256)} %param.23) | copy-start | bytes 1684
  12.3 49.7 %collective-permute-start = (f32[2,30,32,1]{2,0,3,1:T(2,128)S(1)}, f32[2,30,32,1]{2,0,3,1:T(2,128)S(1)}, u32[]{:S(2)}, u32[]{:S(2)}) collective-permute-start(f32[2,30,32,1]{2,0,3,1:T(2,128)S(1)} %copy.52), channel_id=1, source_target_pairs={{0,8},{8,16},{16,24},{24,32},{32,40},{40,48},{48,56},{56,64},{64,7... | collective-permute-start | bytes 23048 | tf_op jit(solution)/shard_map/ppermute | solution.py:17
  18.0 43.1 %collective-permute-start.1 = (f32[2,30,32,1]{2,0,3,1:T(2,128)S(1)}, f32[2,30,32,1]{2,0,3,1:T(2,128)S(1)}, u32[]{:S(2)}, u32[]{:S(2)}) collective-permute-start(f32[2,30,32,1]{2,0,3,1:T(2,128)S(1)} %copy.53), channel_id=1, source_target_pairs={{8,0},{16,8},{24,16},{32,24},{40,32},{48,40},{56,48},{64,56},{72,6... | collective-permute-start | bytes 23048 | tf_op jit(solution)/shard_map/ppermute | solution.py:20
  63.2 9.1 %collective-permute-start.2 = (f32[2,30,1,130]{3,1,2,0:T(8,128)S(1)}, f32[2,30,1,130]{3,1,2,0:T(8,128)S(1)}, u32[]{:S(2)}, u32[]{:S(2)}) collective-permute-start(f32[2,30,1,130]{3,1,2,0:T(8,128)S(1)} %get-tuple-element.348), channel_id=1, source_target_pairs={{1,0},{2,1},{3,2},{4,3},{5,4},{6,5},{7,6},{9,8},{10,9},{11,10},{12... | collective-permute-start | bytes 93608 | tf_op jit(solution)/shard_map/ppermute | solution.py:20
  64.5 9.5 %collective-permute-start.3 = (f32[2,30,1,130]{3,1,2,0:T(8,128)S(1)}, f32[2,30,1,130]{3,1,2,0:T(8,128)S(1)}, u32[]{:S(2)}, u32[]{:S(2)}) collective-permute-start(f32[2,30,1,130]{3,1,2,0:T(8,128)S(1)} %get-tuple-element.349), channel_id=1, source_target_pairs={{0,1},{1,2},{2,3},{3,4},{4,5},{5,6},{6,7},{8,9},{9,10},{10,11},{11... | collective-permute-start | bytes 93608 | tf_op jit(solution)/shard_map/ppermute | solution.py:17
  99.3 4.0 copy-start.5
  99.4 6.7 %copy-start.7 = (f32[140]{0:T(256)S(1)}, f32[140]{0:T(256)}, u32[]{:S(2)}) copy-start(f32[140]{0:T(256)} %param.21) | copy-start | bytes 1684
  615.8 19.2 %all-to-all-start = ((f32[16,4,30,128]{3,1,2,0:T(4,128)}), f32[16,4,30,128]{3,1,2,0:T(4,128)S(1)}, u32[]{:S(2)}, u32[]{:S(2)}) async-start(f32[16,4,30,128]{3,1,2,0:T(4,128)} %copy.61), calls=%async_computation | async-start | bytes 1966080 | tf_op jit(solution)/shard_map/all_to_all | solution.py:190
  622.1 13.6 %copy-start = (f32[2,30,32,128]{3,1,2,0:T(8,128)S(1)}, f32[2,30,32,128]{3,1,2,0:T(8,128)}, u32[]{:S(2)}) copy-start(f32[2,30,32,128]{3,1,2,0:T(8,128)} %fusion.25) | copy-start | bytes 2949124
Sparse Core Ops, SparseCore 0:
  10.8 77.1 all-gather.2
where the time goes:
time: 645 us; the launch traced here: 644 us
  matrix products  423 us (66%)
  other arithmetic  97.6 us (15%)
  blocking collectives  37.5 us (6%)
  local copies, waits for them, and re-layouts  27.6 us (4%)
  waiting for transfers between devices  23 us (4%)
  starting transfers between devices  18.2 us (3%)
  between operations  14.4 us (2%)
    dot_general x60, matrix products, optical_depth(): jnp.dot(table_layer, weights, preferred_element_type=jnp.float32)  417 us
    min x30, other arithmetic, optical_depth(): temp_pos = jnp.clip((air_temp + 3.0) * ((NT - 1.0) / 6.0), 0.0, NT - 1.0)  36.2 us
    add x30, other arithmetic, downward(): source = planck_emission_factor[:, None] * (1.0 + 0.25 * layer[0][None, :])  36.1 us
    all_gather x1, blocking collectives, on_device(): lax.all_gather(own_hosts[None], 'gx', axis=0, tiled=True)  20.2 us
    all_gather x1, blocking collectives, on_device(): lax.all_gather(light[None], 'gx', axis=0, tiled=True)  17.3 us
  transfers between devices with their start and end apart: 6, of which 4 were waited for; matrix products, arithmetic and copies ran while one was open for 3% of the time, Pallas kernels for 0%

commit v1 on v0

--- a/solution.py
+++ b/solution.py
@@ -169,7 +169,9 @@
     every_state, every_light, every_host = (
         lax.all_gather(prognostic_bundle[None], "gx", axis=0, tiled=True),
         lax.all_gather(light[None], "gx", axis=0, tiled=True),
-        lax.all_gather(own_hosts[None], "gx", axis=0, tiled=True),
+        jnp.concatenate(
+            lax.all_to_all(jnp.stack([own_hosts[None]] * lax.axis_size("gx")), "gx", 0, 0), axis=0
+        ),
     )
     mine = jnp.reshape(lax.axis_index("gx"), (1,))
     chooser = slot_table(every_host, mine, capacity)[:, 0].astype(jnp.bfloat16)

time: 645 us -> 645 us (level)
  blocking collectives: 37.5 us -> 21.1 us
  waiting for transfers between devices: 23 us -> 32.4 us
    all_gather x1 -> x0, blocking collectives: 20.2 us -> none  [on_device(): lax.all_gather(own_hosts[None], 'gx', axis=0, tiled=True)]
    all_gather x1, waiting for transfers between devices: 11.5 us -> 20.9 us  [on_device(): lax.all_gather(prognostic_bundle[None], 'gx', axis=0, tiled=True)]
    all_to_all x0 -> x1, starting transfers between devices: none -> 7.34 us  [on_device(): lax.all_to_all(jnp.stack([own_hosts[None]] * lax.axis_size('gx')), 'gx',...]
  transfers between devices with their start and end apart: 6 -> 7, of which waited for: 4 -> 4; matrix products, arithmetic and copies ran while one was open for 3% -> 3% of each run, Pallas kernels for 0% -> 0%
where the time goes in v1:
time: 645 us; the launch traced here: 643 us
  matrix products  423 us (66%)
  other arithmetic  97.3 us (15%)
  waiting for transfers between devices  32.4 us (5%)
  local copies, waits for them, and re-layouts  28.9 us (4%)
  starting transfers between devices  24.5 us (4%)
  blocking collectives  21.1 us (3%)
  between operations  14.4 us (2%)
    dot_general x60, matrix products, optical_depth(): jnp.dot(table_layer, weights, preferred_element_type=jnp.float32)  417 us
    min x30, other arithmetic, optical_depth(): temp_pos = jnp.clip((air_temp + 3.0) * ((NT - 1.0) / 6.0), 0.0, NT - 1.0)  36 us
    add x30, other arithmetic, downward(): source = planck_emission_factor[:, None] * (1.0 + 0.25 * layer[0][None, :])  36 us
    all_gather x1, blocking collectives, on_device(): lax.all_gather(light[None], 'gx', axis=0, tiled=True)  21.1 us
    all_gather x1, waiting for transfers between devices, on_device(): lax.all_gather(prognostic_bundle[None], 'gx', axis=0, tiled=True)  20.9 us
  transfers between devices with their start and end apart: 7, of which 4 were waited for; matrix products, arithmetic and copies ran while one was open for 3% of the time, Pallas kernels for 0%

profile of v1, /device:TPU:1, one launch (start us, length us, event | category | flops | bytes accessed | tf_op | source)
XLA Modules:
  0.0 643.5 jit_solution(16156209815414205394)
XLA Ops:
  11.9 7.3 %all-to-all-start = ((s32[16,1,32]{2,1,0:T(1,128)}), s32[16,1,32]{2,1,0:T(1,128)S(1)}, u32[]{:S(2)}, u32[]{:S(2)}) async-start(s32[16,1,32]{2,1,0:T(1,128)} %stack.36), calls=%async_computation | async-start | bytes 16384 | tf_op jit(solution)/shard_map/all_to_all | solution.py:173
  27.4 21.1 %all_gather.6 = bf16[16,2,32,128]{3,2,1,0:T(8,128)(2,1)S(1)} all-gather(bf16[1,2,32,128]{3,2,1,0:T(8,128)(2,1)S(1)} %pad_maximum_fusion.18), channel_id=1, replica_groups=mesh['gx'=16,'gy'=8] {'gx'}, dimensions={0}, use_global_device_ids=true | all-gather | bytes 278528 | tf_op jit(solution)/shard_map/all_gather | solution.py:171
  55.3 5.8 collective-permute-start.3
  67.3 20.9 %all-gather.2.cloned.1.call-done = bf16[16,3,30,32,128]{4,3,2,1,0:T(8,128)(2,1)} async-done(((bf16[1,3,30,32,128]{4,3,2,1,0:T(8,128)(2,1)}), bf16[16,3,30,32,128]{4,3,2,1,0:T(8,128)(2,1)}) %all-gather.2.cloned.1.call-update) | async-done | bytes 11796496 | tf_op jit(solution)/shard_map/all_gather | solution.py:170
  88.2 6.0 convert_bitcast_fusion
  106.4 213.2 %while.31 = (s32[]{:T(128)}, f32[140,8192]{1,0:T(8,128)}, f32[30,8192]{1,0:T(8,128)S(1)}, bf16[30,140,128]{2,1,0:T(8,128)(2,1)}, f32[30,3,8192]{2,1,0:T(4,128)},...) while((s32[]{:T(128)}, f32[140,8192]{1,0:T(8,128)}, ...), condition=%wide.region_6.7_spmd, body=%wide.region_4.6_spmd.sunk | while | flops 308002816 | bytes 11375885 | solution.py:88
  107.7 5.6 subtract_reduce_fusion.4
  114.8 5.6 subtract_reduce_fusion.4
  121.9 5.6 subtract_reduce_fusion.4
  129.0 5.6 subtract_reduce_fusion.4
  136.2 5.6 subtract_reduce_fusion.4
  143.3 5.6 subtract_reduce_fusion.4
  150.4 5.6 subtract_reduce_fusion.4
  157.5 5.6 subtract_reduce_fusion.4
  164.6 5.6 subtract_reduce_fusion.4
  178.8 5.6 subtract_reduce_fusion.4
  185.9 5.6 subtract_reduce_fusion.4
  193.0 5.6 subtract_reduce_fusion.4
  200.1 5.6 subtract_reduce_fusion.4
  207.2 5.6 subtract_reduce_fusion.4
  221.4 5.6 subtract_reduce_fusion.4
  228.6 5.6 subtract_reduce_fusion.4
  235.7 5.6 subtract_reduce_fusion.4
  242.8 5.6 subtract_reduce_fusion.4
  257.0 5.6 subtract_reduce_fusion.4
  264.1 5.6 subtract_reduce_fusion.4
  271.2 5.6 subtract_reduce_fusion.4
  278.3 5.6 subtract_reduce_fusion.4
  292.5 5.6 subtract_reduce_fusion.4
  299.6 5.6 subtract_reduce_fusion.4
  306.7 5.6 subtract_reduce_fusion.4
  313.8 5.6 subtract_reduce_fusion.4
  319.6 293.7 %while.32 = (s32[]{:T(128)}, f32[140,8192]{1,0:T(8,128)}, f32[140,8192]{1,0:T(8,128)}, f32[30,8192]{1,0:T(8,128)S(1)}, bf16[30,140,128]{2,1,0:T(8,128)(2,1)}, /*...) while((s32[]{:T(128)}, f32[140,8192]{1,0:T(8,128)}, ...), condition=%wide.region_3.4_spmd.clone, body=%wide.region_1.3_spmd.clone.sunk | while | flops 314884096 | bytes 20714776 | solution.py:84
  321.0 7.6 %subtract_reduce_fusion.5 = (f32[8192]{0:T(1024)S(1)}, f32[140,8192]{1,0:T(8,128)}, f32[140,8192]{1,0:T(8,128)}) fusion(f32[140,8192]{1,0:T(8,128)} %get-tuple-element.499, f32[140,8192]{1,0:T(8,128)} %get-tuple-element.498, pred[]{:T(512)S(6)} %compare.3, f32[8192]{0:T(1024)S(1)} %get-tuple-element.518, f32[8192]{0:T(1024)S(1)} %bitcast.125, ...), kind=kOutput, calls=%fused_computation.21.clone.1 | convolution fusion | flops 314040320 | bytes 19567716 | tf_op jit(solution)/shard_map/while/body/eval_jaxpr/dot_general | solution.py:47
  330.1 8.3 %subtract_reduce_fusion.5 = (f32[8192]{0:T(1024)S(1)}, f32[140,8192]{1,0:T(8,128)}, f32[140,8192]{1,0:T(8,128)}) fusion(f32[140,8192]{1,0:T(8,128)} %get-tuple-element.499, f32[140,8192]{1,0:T(8,128)} %get-tuple-element.498, pred[]{:T(512)S(6)} %compare.3, f32[8192]{0:T(1024)S(1)} %get-tuple-element.518, f32[8192]{0:T(1024)S(1)} %bitcast.125, ...), kind=kOutput, calls=%fused_computation.21.clone.1 | convolution fusion | flops 314040320 | bytes 19567716 | tf_op jit(solution)/shard_map/while/body/eval_jaxpr/dot_general | solution.py:47
  339.9 8.3 %subtract_reduce_fusion.5 = (f32[8192]{0:T(1024)S(1)}, f32[140,8192]{1,0:T(8,128)}, f32[140,8192]{1,0:T(8,128)}) fusion(f32[140,8192]{1,0:T(8,128)} %get-tuple-element.499, f32[140,8192]{1,0:T(8,128)} %get-tuple-element.498, pred[]{:T(512)S(6)} %compare.3, f32[8192]{0:T(1024)S(1)} %get-tuple-element.518, f32[8192]{0:T(1024)S(1)} %bitcast.125, ...), kind=kOutput, calls=%fused_computation.21.clone.1 | convolution fusion | flops 314040320 | bytes 19567716 | tf_op jit(solution)/shard_map/while/body/eval_jaxpr/dot_general | solution.py:47
  349.7 8.3 %subtract_reduce_fusion.5 = (f32[8192]{0:T(1024)S(1)}, f32[140,8192]{1,0:T(8,128)}, f32[140,8192]{1,0:T(8,128)}) fusion(f32[140,8192]{1,0:T(8,128)} %get-tuple-element.499, f32[140,8192]{1,0:T(8,128)} %get-tuple-element.498, pred[]{:T(512)S(6)} %compare.3, f32[8192]{0:T(1024)S(1)} %get-tuple-element.518, f32[8192]{0:T(1024)S(1)} %bitcast.125, ...), kind=kOutput, calls=%fused_computation.21.clone.1 | convolution fusion | flops 314040320 | bytes 19567716 | tf_op jit(solution)/shard_map/while/body/eval_jaxpr/dot_general | solution.py:47
  359.5 8.3 %subtract_reduce_fusion.5 = (f32[8192]{0:T(1024)S(1)}, f32[140,8192]{1,0:T(8,128)}, f32[140,8192]{1,0:T(8,128)}) fusion(f32[140,8192]{1,0:T(8,128)} %get-tuple-element.499, f32[140,8192]{1,0:T(8,128)} %get-tuple-element.498, pred[]{:T(512)S(6)} %compare.3, f32[8192]{0:T(1024)S(1)} %get-tuple-element.518, f32[8192]{0:T(1024)S(1)} %bitcast.125, ...), kind=kOutput, calls=%fused_computation.21.clone.1 | convolution fusion | flops 314040320 | bytes 19567716 | tf_op jit(solution)/shard_map/while/body/eval_jaxpr/dot_general | solution.py:47
  369.3 8.3 %subtract_reduce_fusion.5 = (f32[8192]{0:T(1024)S(1)}, f32[140,8192]{1,0:T(8,128)}, f32[140,8192]{1,0:T(8,128)}) fusion(f32[140,8192]{1,0:T(8,128)} %get-tuple-element.499, f32[140,8192]{1,0:T(8,128)} %get-tuple-element.498, pred[]{:T(512)S(6)} %compare.3, f32[8192]{0:T(1024)S(1)} %get-tuple-element.518, f32[8192]{0:T(1024)S(1)} %bitcast.125, ...), kind=kOutput, calls=%fused_computation.21.clone.1 | convolution fusion | flops 314040320 | bytes 19567716 | tf_op jit(solution)/shard_map/while/body/eval_jaxpr/dot_general | solution.py:47
  379.1 8.3 %subtract_reduce_fusion.5 = (f32[8192]{0:T(1024)S(1)}, f32[140,8192]{1,0:T(8,128)}, f32[140,8192]{1,0:T(8,128)}) fusion(f32[140,8192]{1,0:T(8,128)} %get-tuple-element.499, f32[140,8192]{1,0:T(8,128)} %get-tuple-element.498, pred[]{:T(512)S(6)} %compare.3, f32[8192]{0:T(1024)S(1)} %get-tuple-element.518, f32[8192]{0:T(1024)S(1)} %bitcast.125, ...), kind=kOutput, calls=%fused_computation.21.clone.1 | convolution fusion | flops 314040320 | bytes 19567716 | tf_op jit(solution)/shard_map/while/body/eval_jaxpr/dot_general | solution.py:47
  388.9 8.3 %subtract_reduce_fusion.5 = (f32[8192]{0:T(1024)S(1)}, f32[140,8192]{1,0:T(8,128)}, f32[140,8192]{1,0:T(8,128)}) fusion(f32[140,8192]{1,0:T(8,128)} %get-tuple-element.499, f32[140,8192]{1,0:T(8,128)} %get-tuple-element.498, pred[]{:T(512)S(6)} %compare.3, f32[8192]{0:T(1024)S(1)} %get-tuple-element.518, f32[8192]{0:T(1024)S(1)} %bitcast.125, ...), kind=kOutput, calls=%fused_computation.21.clone.1 | convolution fusion | flops 314040320 | bytes 19567716 | tf_op jit(solution)/shard_map/while/body/eval_jaxpr/dot_general | solution.py:47
  398.7 8.3 %subtract_reduce_fusion.5 = (f32[8192]{0:T(1024)S(1)}, f32[140,8192]{1,0:T(8,128)}, f32[140,8192]{1,0:T(8,128)}) fusion(f32[140,8192]{1,0:T(8,128)} %get-tuple-element.499, f32[140,8192]{1,0:T(8,128)} %get-tuple-element.498, pred[]{:T(512)S(6)} %compare.3, f32[8192]{0:T(1024)S(1)} %get-tuple-element.518, f32[8192]{0:T(1024)S(1)} %bitcast.125, ...), kind=kOutput, calls=%fused_computation.21.clone.1 | convolution fusion | flops 314040320 | bytes 19567716 | tf_op jit(solution)/shard_map/while/body/eval_jaxpr/dot_general | solution.py:47
  408.6 8.3 %subtract_reduce_fusion.5 = (f32[8192]{0:T(1024)S(1)}, f32[140,8192]{1,0:T(8,128)}, f32[140,8192]{1,0:T(8,128)}) fusion(f32[140,8192]{1,0:T(8,128)} %get-tuple-element.499, f32[140,8192]{1,0:T(8,128)} %get-tuple-element.498, pred[]{:T(512)S(6)} %compare.3, f32[8192]{0:T(1024)S(1)} %get-tuple-element.518, f32[8192]{0:T(1024)S(1)} %bitcast.125, ...), kind=kOutput, calls=%fused_computation.21.clone.1 | convolution fusion | flops 314040320 | bytes 19567716 | tf_op jit(solution)/shard_map/while/body/eval_jaxpr/dot_general | solution.py:47
  418.4 8.3 %subtract_reduce_fusion.5 = (f32[8192]{0:T(1024)S(1)}, f32[140,8192]{1,0:T(8,128)}, f32[140,8192]{1,0:T(8,128)}) fusion(f32[140,8192]{1,0:T(8,128)} %get-tuple-element.499, f32[140,8192]{1,0:T(8,128)} %get-tuple-element.498, pred[]{:T(512)S(6)} %compare.3, f32[8192]{0:T(1024)S(1)} %get-tuple-element.518, f32[8192]{0:T(1024)S(1)} %bitcast.125, ...), kind=kOutput, calls=%fused_computation.21.clone.1 | convolution fusion | flops 314040320 | bytes 19567716 | tf_op jit(solution)/shard_map/while/body/eval_jaxpr/dot_general | solution.py:47
  428.2 8.3 %subtract_reduce_fusion.5 = (f32[8192]{0:T(1024)S(1)}, f32[140,8192]{1,0:T(8,128)}, f32[140,8192]{1,0:T(8,128)}) fusion(f32[140,8192]{1,0:T(8,128)} %get-tuple-element.499, f32[140,8192]{1,0:T(8,128)} %get-tuple-element.498, pred[]{:T(512)S(6)} %compare.3, f32[8192]{0:T(1024)S(1)} %get-tuple-element.518, f32[8192]{0:T(1024)S(1)} %bitcast.125, ...), kind=kOutput, calls=%fused_computation.21.clone.1 | convolution fusion | flops 314040320 | bytes 19567716 | tf_op jit(solution)/shard_map/while/body/eval_jaxpr/dot_general | solution.py:47
  438.0 8.3 %subtract_reduce_fusion.5 = (f32[8192]{0:T(1024)S(1)}, f32[140,8192]{1,0:T(8,128)}, f32[140,8192]{1,0:T(8,128)}) fusion(f32[140,8192]{1,0:T(8,128)} %get-tuple-element.499, f32[140,8192]{1,0:T(8,128)} %get-tuple-element.498, pred[]{:T(512)S(6)} %compare.3, f32[8192]{0:T(1024)S(1)} %get-tuple-element.518, f32[8192]{0:T(1024)S(1)} %bitcast.125, ...), kind=kOutput, calls=%fused_computation.21.clone.1 | convolution fusion | flops 314040320 | bytes 19567716 | tf_op jit(solution)/shard_map/while/body/eval_jaxpr/dot_general | solution.py:47
  447.8 8.3 %subtract_reduce_fusion.5 = (f32[8192]{0:T(1024)S(1)}, f32[140,8192]{1,0:T(8,128)}, f32[140,8192]{1,0:T(8,128)}) fusion(f32[140,8192]{1,0:T(8,128)} %get-tuple-element.499, f32[140,8192]{1,0:T(8,128)} %get-tuple-element.498, pred[]{:T(512)S(6)} %compare.3, f32[8192]{0:T(1024)S(1)} %get-tuple-element.518, f32[8192]{0:T(1024)S(1)} %bitcast.125, ...), kind=kOutput, calls=%fused_computation.21.clone.1 | convolution fusion | flops 314040320 | bytes 19567716 | tf_op jit(solution)/shard_map/while/body/eval_jaxpr/dot_general | solution.py:47
  457.6 8.3 %subtract_reduce_fusion.5 = (f32[8192]{0:T(1024)S(1)}, f32[140,8192]{1,0:T(8,128)}, f32[140,8192]{1,0:T(8,128)}) fusion(f32[140,8192]{1,0:T(8,128)} %get-tuple-element.499, f32[140,8192]{1,0:T(8,128)} %get-tuple-element.498, pred[]{:T(512)S(6)} %compare.3, f32[8192]{0:T(1024)S(1)} %get-tuple-element.518, f32[8192]{0:T(1024)S(1)} %bitcast.125, ...), kind=kOutput, calls=%fused_computation.21.clone.1 | convolution fusion | flops 314040320 | bytes 19567716 | tf_op jit(solution)/shard_map/while/body/eval_jaxpr/dot_general | solution.py:47
  467.4 8.3 %subtract_reduce_fusion.5 = (f32[8192]{0:T(1024)S(1)}, f32[140,8192]{1,0:T(8,128)}, f32[140,8192]{1,0:T(8,128)}) fusion(f32[140,8192]{1,0:T(8,128)} %get-tuple-element.499, f32[140,8192]{1,0:T(8,128)} %get-tuple-element.498, pred[]{:T(512)S(6)} %compare.3, f32[8192]{0:T(1024)S(1)} %get-tuple-element.518, f32[8192]{0:T(1024)S(1)} %bitcast.125, ...), kind=kOutput, calls=%fused_computation.21.clone.1 | convolution fusion | flops 314040320 | bytes 19567716 | tf_op jit(solution)/shard_map/while/body/eval_jaxpr/dot_general | solution.py:47
  477.3 8.3 %subtract_reduce_fusion.5 = (f32[8192]{0:T(1024)S(1)}, f32[140,8192]{1,0:T(8,128)}, f32[140,8192]{1,0:T(8,128)}) fusion(f32[140,8192]{1,0:T(8,128)} %get-tuple-element.499, f32[140,8192]{1,0:T(8,128)} %get-tuple-element.498, pred[]{:T(512)S(6)} %compare.3, f32[8192]{0:T(1024)S(1)} %get-tuple-element.518, f32[8192]{0:T(1024)S(1)} %bitcast.125, ...), kind=kOutput, calls=%fused_computation.21.clone.1 | convolution fusion | flops 314040320 | bytes 19567716 | tf_op jit(solution)/shard_map/while/body/eval_jaxpr/dot_general | solution.py:47
  487.1 8.3 %subtract_reduce_fusion.5 = (f32[8192]{0:T(1024)S(1)}, f32[140,8192]{1,0:T(8,128)}, f32[140,8192]{1,0:T(8,128)}) fusion(f32[140,8192]{1,0:T(8,128)} %get-tuple-element.499, f32[140,8192]{1,0:T(8,128)} %get-tuple-element.498, pred[]{:T(512)S(6)} %compare.3, f32[8192]{0:T(1024)S(1)} %get-tuple-element.518, f32[8192]{0:T(1024)S(1)} %bitcast.125, ...), kind=kOutput, calls=%fused_computation.21.clone.1 | convolution fusion | flops 314040320 | bytes 19567716 | tf_op jit(solution)/shard_map/while/body/eval_jaxpr/dot_general | solution.py:47
  496.9 8.3 %subtract_reduce_fusion.5 = (f32[8192]{0:T(1024)S(1)}, f32[140,8192]{1,0:T(8,128)}, f32[140,8192]{1,0:T(8,128)}) fusion(f32[140,8192]{1,0:T(8,128)} %get-tuple-element.499, f32[140,8192]{1,0:T(8,128)} %get-tuple-element.498, pred[]{:T(512)S(6)} %compare.3, f32[8192]{0:T(1024)S(1)} %get-tuple-element.518, f32[8192]{0:T(1024)S(1)} %bitcast.125, ...), kind=kOutput, calls=%fused_computation.21.clone.1 | convolution fusion | flops 314040320 | bytes 19567716 | tf_op jit(solution)/shard_map/while/body/eval_jaxpr/dot_general | solution.py:47
  506.7 8.3 %subtract_reduce_fusion.5 = (f32[8192]{0:T(1024)S(1)}, f32[140,8192]{1,0:T(8,128)}, f32[140,8192]{1,0:T(8,128)}) fusion(f32[140,8192]{1,0:T(8,128)} %get-tuple-element.499, f32[140,8192]{1,0:T(8,128)} %get-tuple-element.498, pred[]{:T(512)S(6)} %compare.3, f32[8192]{0:T(1024)S(1)} %get-tuple-element.518, f32[8192]{0:T(1024)S(1)} %bitcast.125, ...), kind=kOutput, calls=%fused_computation.21.clone.1 | convolution fusion | flops 314040320 | bytes 19567716 | tf_op jit(solution)/shard_map/while/body/eval_jaxpr/dot_general | solution.py:47
  516.5 8.3 %subtract_reduce_fusion.5 = (f32[8192]{0:T(1024)S(1)}, f32[140,8192]{1,0:T(8,128)}, f32[140,8192]{1,0:T(8,128)}) fusion(f32[140,8192]{1,0:T(8,128)} %get-tuple-element.499, f32[140,8192]{1,0:T(8,128)} %get-tuple-element.498, pred[]{:T(512)S(6)} %compare.3, f32[8192]{0:T(1024)S(1)} %get-tuple-element.518, f32[8192]{0:T(1024)S(1)} %bitcast.125, ...), kind=kOutput, calls=%fused_computation.21.clone.1 | convolution fusion | flops 314040320 | bytes 19567716 | tf_op jit(solution)/shard_map/while/body/eval_jaxpr/dot_general | solution.py:47
  526.3 8.3 %subtract_reduce_fusion.5 = (f32[8192]{0:T(1024)S(1)}, f32[140,8192]{1,0:T(8,128)}, f32[140,8192]{1,0:T(8,128)}) fusion(f32[140,8192]{1,0:T(8,128)} %get-tuple-element.499, f32[140,8192]{1,0:T(8,128)} %get-tuple-element.498, pred[]{:T(512)S(6)} %compare.3, f32[8192]{0:T(1024)S(1)} %get-tuple-element.518, f32[8192]{0:T(1024)S(1)} %bitcast.125, ...), kind=kOutput, calls=%fused_computation.21.clone.1 | convolution fusion | flops 314040320 | bytes 19567716 | tf_op jit(solution)/shard_map/while/body/eval_jaxpr/dot_general | solution.py:47
  536.2 8.3 %subtract_reduce_fusion.5 = (f32[8192]{0:T(1024)S(1)}, f32[140,8192]{1,0:T(8,128)}, f32[140,8192]{1,0:T(8,128)}) fusion(f32[140,8192]{1,0:T(8,128)} %get-tuple-element.499, f32[140,8192]{1,0:T(8,128)} %get-tuple-element.498, pred[]{:T(512)S(6)} %compare.3, f32[8192]{0:T(1024)S(1)} %get-tuple-element.518, f32[8192]{0:T(1024)S(1)} %bitcast.125, ...), kind=kOutput, calls=%fused_computation.21.clone.1 | convolution fusion | flops 314040320 | bytes 19567716 | tf_op jit(solution)/shard_map/while/body/eval_jaxpr/dot_general | solution.py:47
  546.0 8.3 %subtract_reduce_fusion.5 = (f32[8192]{0:T(1024)S(1)}, f32[140,8192]{1,0:T(8,128)}, f32[140,8192]{1,0:T(8,128)}) fusion(f32[140,8192]{1,0:T(8,128)} %get-tuple-element.499, f32[140,8192]{1,0:T(8,128)} %get-tuple-element.498, pred[]{:T(512)S(6)} %compare.3, f32[8192]{0:T(1024)S(1)} %get-tuple-element.518, f32[8192]{0:T(1024)S(1)} %bitcast.125, ...), kind=kOutput, calls=%fused_computation.21.clone.1 | convolution fusion | flops 314040320 | bytes 19567716 | tf_op jit(solution)/shard_map/while/body/eval_jaxpr/dot_general | solution.py:47
  555.8 8.3 %subtract_reduce_fusion.5 = (f32[8192]{0:T(1024)S(1)}, f32[140,8192]{1,0:T(8,128)}, f32[140,8192]{1,0:T(8,128)}) fusion(f32[140,8192]{1,0:T(8,128)} %get-tuple-element.499, f32[140,8192]{1,0:T(8,128)} %get-tuple-element.498, pred[]{:T(512)S(6)} %compare.3, f32[8192]{0:T(1024)S(1)} %get-tuple-element.518, f32[8192]{0:T(1024)S(1)} %bitcast.125, ...), kind=kOutput, calls=%fused_computation.21.clone.1 | convolution fusion | flops 314040320 | bytes 19567716 | tf_op jit(solution)/shard_map/while/body/eval_jaxpr/dot_general | solution.py:47
  565.6 8.3 %subtract_reduce_fusion.5 = (f32[8192]{0:T(1024)S(1)}, f32[140,8192]{1,0:T(8,128)}, f32[140,8192]{1,0:T(8,128)}) fusion(f32[140,8192]{1,0:T(8,128)} %get-tuple-element.499, f32[140,8192]{1,0:T(8,128)} %get-tuple-element.498, pred[]{:T(512)S(6)} %compare.3, f32[8192]{0:T(1024)S(1)} %get-tuple-element.518, f32[8192]{0:T(1024)S(1)} %bitcast.125, ...), kind=kOutput, calls=%fused_computation.21.clone.1 | convolution fusion | flops 314040320 | bytes 19567716 | tf_op jit(solution)/shard_map/while/body/eval_jaxpr/dot_general | solution.py:47
  575.4 8.3 %subtract_reduce_fusion.5 = (f32[8192]{0:T(1024)S(1)}, f32[140,8192]{1,0:T(8,128)}, f32[140,8192]{1,0:T(8,128)}) fusion(f32[140,8192]{1,0:T(8,128)} %get-tuple-element.499, f32[140,8192]{1,0:T(8,128)} %get-tuple-element.498, pred[]{:T(512)S(6)} %compare.3, f32[8192]{0:T(1024)S(1)} %get-tuple-element.518, f32[8192]{0:T(1024)S(1)} %bitcast.125, ...), kind=kOutput, calls=%fused_computation.21.clone.1 | convolution fusion | flops 314040320 | bytes 19567716 | tf_op jit(solution)/shard_map/while/body/eval_jaxpr/dot_general | solution.py:47
  585.2 8.3 %subtract_reduce_fusion.5 = (f32[8192]{0:T(1024)S(1)}, f32[140,8192]{1,0:T(8,128)}, f32[140,8192]{1,0:T(8,128)}) fusion(f32[140,8192]{1,0:T(8,128)} %get-tuple-element.499, f32[140,8192]{1,0:T(8,128)} %get-tuple-element.498, pred[]{:T(512)S(6)} %compare.3, f32[8192]{0:T(1024)S(1)} %get-tuple-element.518, f32[8192]{0:T(1024)S(1)} %bitcast.125, ...), kind=kOutput, calls=%fused_computation.21.clone.1 | convolution fusion | flops 314040320 | bytes 19567716 | tf_op jit(solution)/shard_map/while/body/eval_jaxpr/dot_general | solution.py:47
  595.0 8.3 %subtract_reduce_fusion.5 = (f32[8192]{0:T(1024)S(1)}, f32[140,8192]{1,0:T(8,128)}, f32[140,8192]{1,0:T(8,128)}) fusion(f32[140,8192]{1,0:T(8,128)} %get-tuple-element.499, f32[140,8192]{1,0:T(8,128)} %get-tuple-element.498, pred[]{:T(512)S(6)} %compare.3, f32[8192]{0:T(1024)S(1)} %get-tuple-element.518, f32[8192]{0:T(1024)S(1)} %bitcast.125, ...), kind=kOutput, calls=%fused_computation.21.clone.1 | convolution fusion | flops 314040320 | bytes 19567716 | tf_op jit(solution)/shard_map/while/body/eval_jaxpr/dot_general | solution.py:47
  604.9 8.3 %subtract_reduce_fusion.5 = (f32[8192]{0:T(1024)S(1)}, f32[140,8192]{1,0:T(8,128)}, f32[140,8192]{1,0:T(8,128)}) fusion(f32[140,8192]{1,0:T(8,128)} %get-tuple-element.499, f32[140,8192]{1,0:T(8,128)} %get-tuple-element.498, pred[]{:T(512)S(6)} %compare.3, f32[8192]{0:T(1024)S(1)} %get-tuple-element.518, f32[8192]{0:T(1024)S(1)} %bitcast.125, ...), kind=kOutput, calls=%fused_computation.21.clone.1 | convolution fusion | flops 314040320 | bytes 19567716 | tf_op jit(solution)/shard_map/while/body/eval_jaxpr/dot_general | solution.py:47
  626.9 7.8 %all-to-all-done.1 = f32[16,4,30,128]{3,1,2,0:T(4,128)S(1)} async-done(((f32[16,4,30,128]{3,1,2,0:T(4,128)}), f32[16,4,30,128]{3,1,2,0:T(4,128)S(1)}, u32[]{:S(2)}, u32[]{:S(2)}) %all-to-all-start.1) | async-done | bytes 983072 | tf_op jit(solution)/shard_map/all_to_all | solution.py:192
  (318 shorter events, 163.7 us)
Async XLA Ops:
  7.2 12.1 %copy-start.1 = (f32[30,32,128]{2,1,0:T(8,128)S(1)}, f32[30,32,128]{2,1,0:T(8,128)}, u32[]{:S(2)}) copy-start(f32[30,32,128]{2,1,0:T(8,128)} %param.15) | copy-start | bytes 1474564
  7.2 12.1 %copy-start.2 = (f32[30,32,128]{2,1,0:T(8,128)S(1)}, f32[30,32,128]{2,1,0:T(8,128)}, u32[]{:S(2)}) copy-start(f32[30,32,128]{2,1,0:T(8,128)} %param.14) | copy-start | bytes 1474564
  7.2 81.1 %all-gather.2.cloned.1.call-start = ((), (), s32[]{:S(2)}) async-start(), calls=%async_computation.2 | async-start | bytes 12533760 | tf_op jit(solution)/shard_map/all_gather | solution.py:170
  9.6 17.5 %copy-start.8 = (s32[1,32]{1,0:T(1,128)S(1)}, s32[1,32]{1,0:T(1,128)}, u32[]{:S(2)}) copy-start(s32[1,32]{1,0:T(1,128)} %param.18) | copy-start | bytes 388
  9.7 17.5 %copy-start.3 = (f32[32,128]{1,0:T(8,128)S(1)}, f32[32,128]{1,0:T(8,128)}, u32[]{:S(2)}) copy-start(f32[32,128]{1,0:T(8,128)} %param.17) | copy-start | bytes 49156
  9.7 17.5 %copy-start.6 = (s32[1,32,1]{1,2,0:T(1,128)S(1)}, s32[1,32,1]{1,2,0:T(1,128)}, u32[]{:S(2)}) copy-start(s32[1,32,1]{1,2,0:T(1,128)} %param.19) | copy-start | bytes 388
  10.6 38.6 %copy-start.4 = (f32[140]{0:T(256)S(1)}, f32[140]{0:T(256)}, u32[]{:S(2)}) copy-start(f32[140]{0:T(256)} %param.23) | copy-start | bytes 1684
  11.9 36.6 %all-to-all-start = ((s32[16,1,32]{2,1,0:T(1,128)}), s32[16,1,32]{2,1,0:T(1,128)S(1)}, u32[]{:S(2)}, u32[]{:S(2)}) async-start(s32[16,1,32]{2,1,0:T(1,128)} %stack.36), calls=%async_computation | async-start | bytes 16384 | tf_op jit(solution)/shard_map/all_to_all | solution.py:173
  20.9 31.9 %collective-permute-start = (f32[2,30,32,1]{2,0,3,1:T(2,128)S(1)}, f32[2,30,32,1]{2,0,3,1:T(2,128)S(1)}, u32[]{:S(2)}, u32[]{:S(2)}) collective-permute-start(f32[2,30,32,1]{2,0,3,1:T(2,128)S(1)} %copy.52), channel_id=1, source_target_pairs={{0,8},{8,16},{16,24},{24,32},{32,40},{40,48},{48,56},{56,64},{64,7... | collective-permute-start | bytes 23048 | tf_op jit(solution)/shard_map/ppermute | solution.py:17
  25.2 26.7 %collective-permute-start.1 = (f32[2,30,32,1]{2,0,3,1:T(2,128)S(1)}, f32[2,30,32,1]{2,0,3,1:T(2,128)S(1)}, u32[]{:S(2)}, u32[]{:S(2)}) collective-permute-start(f32[2,30,32,1]{2,0,3,1:T(2,128)S(1)} %copy.53), channel_id=1, source_target_pairs={{8,0},{16,8},{24,16},{32,24},{40,32},{48,40},{56,48},{64,56},{72,6... | collective-permute-start | bytes 23048 | tf_op jit(solution)/shard_map/ppermute | solution.py:20
  54.0 9.1 %collective-permute-start.2 = (f32[2,30,1,130]{3,1,2,0:T(8,128)S(1)}, f32[2,30,1,130]{3,1,2,0:T(8,128)S(1)}, u32[]{:S(2)}, u32[]{:S(2)}) collective-permute-start(f32[2,30,1,130]{3,1,2,0:T(8,128)S(1)} %get-tuple-element.348), channel_id=1, source_target_pairs={{1,0},{2,1},{3,2},{4,3},{5,4},{6,5},{7,6},{9,8},{10,9},{11,10},{12... | collective-permute-start | bytes 93608 | tf_op jit(solution)/shard_map/ppermute | solution.py:20
  55.3 9.5 %collective-permute-start.3 = (f32[2,30,1,130]{3,1,2,0:T(8,128)S(1)}, f32[2,30,1,130]{3,1,2,0:T(8,128)S(1)}, u32[]{:S(2)}, u32[]{:S(2)}) collective-permute-start(f32[2,30,1,130]{3,1,2,0:T(8,128)S(1)} %get-tuple-element.349), channel_id=1, source_target_pairs={{0,1},{1,2},{2,3},{3,4},{4,5},{5,6},{6,7},{8,9},{9,10},{10,11},{11... | collective-permute-start | bytes 93608 | tf_op jit(solution)/shard_map/ppermute | solution.py:17
  99.6 4.0 copy-start.5
  99.6 6.7 %copy-start.7 = (f32[140]{0:T(256)S(1)}, f32[140]{0:T(256)}, u32[]{:S(2)}) copy-start(f32[140]{0:T(256)} %param.21) | copy-start | bytes 1684
  615.2 19.5 %all-to-all-start.1 = ((f32[16,4,30,128]{3,1,2,0:T(4,128)}), f32[16,4,30,128]{3,1,2,0:T(4,128)S(1)}, u32[]{:S(2)}, u32[]{:S(2)}) async-start(f32[16,4,30,128]{3,1,2,0:T(4,128)} %copy.61), calls=%async_computation.1 | async-start | bytes 1966080 | tf_op jit(solution)/shard_map/all_to_all | solution.py:192
  621.9 13.6 %copy-start = (f32[2,30,32,128]{3,1,2,0:T(8,128)S(1)}, f32[2,30,32,128]{3,1,2,0:T(8,128)}, u32[]{:S(2)}) copy-start(f32[2,30,32,128]{3,1,2,0:T(8,128)} %fusion.25) | copy-start | bytes 2949124
Sparse Core Ops, SparseCore 0:
  10.8 77.4 all-gather.1
